TPU v7x, 32 devices: a whole 2x2x4 slice. The times are simulated.
32 devices in a mesh: table: 16 (over z, y, x), score: 2 (over core).
Axes of the slice: x: 2, y: 2, z: 4, core: 2. Of those that a mesh axis runs over, the one named last changes fastest.
Arguments:
- hot_item_table: float32 [2048, 128], replicated, may hold values from -6 to 6
- cold_item_table: float32 [16384, 128], P('table'), may hold values from -6 to 6
- hist_rows: int32 [128, 512], P('table', 'score'), may hold values from 0 to 18431, as said below
- cand_rows: int32 [128, 512], P('table', 'score'), may hold values from 0 to 18431, as said below
- w_query: bfloat16 [128, 128], replicated, may hold values from -0.5 to 0.5
- w_key: bfloat16 [128, 128], replicated, may hold values from -0.5 to 0.5
- w_first: bfloat16 [256, 1024], replicated, may hold values from -0.5 to 0.5
- w_second: bfloat16 [1, 1024, 1024], replicated, may hold values from -0.25 to 0.25
- w_out: bfloat16 [1024], replicated, may hold values from -0.25 to 0.25
Outputs:
- scores: float32 [128, 512], P('table', 'score')
Inputs may be any that keep to these rules, and one draw needn't show every extreme that they name: `hist_rows`: among the history items of one device (8 requests, 256 items each), at most 128 name cold rows of any one owner; for each index along score, one owner is named exactly 128 times by every device along table. `cand_rows`: among the candidates of one device (8 requests, 256 candidates each), at most 128 name cold rows of any one owner; for each index along score, one owner is named exactly 128 times by every device along table.
All inputs are finite; a program needn't handle non-finite values.
Results may differ from a plain program's by a relative error of at most 0.0072.
Values may be sent and summed in bfloat16 or wider, within the bound.
A program may use at most 64 MiB of HBM per device.

v0:
```python
import math
import jax
import jax.numpy as jnp
from jax import lax
from jax.sharding import PartitionSpec as P

H = 512
HOT = 2048
COLD_DEV = 1024


def owner_positions(owner_match):
    item_total, owner_count = owner_match.shape
    block = math.gcd(item_total, 128)
    blocks = item_total // block
    match_bf = owner_match.astype(jnp.bfloat16).reshape(blocks, block, owner_count)
    lower = (
        lax.broadcasted_iota(jnp.int32, (block, block), 0)
        > lax.broadcasted_iota(jnp.int32, (block, block), 1)
    ).astype(jnp.bfloat16)
    within = jnp.einsum("ij,kjo->kio", lower, match_bf, preferred_element_type=jnp.float32)
    totals = jnp.sum(match_bf.astype(jnp.float32), axis=1)
    earlier = (
        lax.broadcasted_iota(jnp.int32, (blocks, blocks), 0)
        > lax.broadcasted_iota(jnp.int32, (blocks, blocks), 1)
    ).astype(jnp.float32)
    offsets = jnp.einsum(
        "bk,ko->bo",
        earlier,
        totals,
        precision=lax.Precision.HIGHEST,
        preferred_element_type=jnp.float32,
    )
    before = (within + offsets[:, None, :]).reshape(item_total, owner_count)
    return jnp.sum(before * owner_match, axis=1).astype(jnp.int32)


def gather_owner_rows(
    grouped_item_codes, owner_capacity_list, hot_item_table, cold_item_table, table_row_count
):
    owner_iota = jnp.arange(table_row_count, dtype=jnp.int32)
    layouts = []
    outgoing = []
    for item_row_codes, slot_capacity in zip(grouped_item_codes, owner_capacity_list):
        is_cold = item_row_codes >= HOT
        relative = jnp.where(is_cold, item_row_codes - HOT, 0)
        owner_id = relative // COLD_DEV
        slot_id = relative % COLD_DEV
        owner_match = jnp.logical_and(
            owner_id[:, None] == owner_iota[None, :], is_cold[:, None]
        ).astype(jnp.float32)
        position = owner_positions(owner_match)
        flat_index = owner_id * slot_capacity + position
        slot_onehot = (
            position[:, None] == jnp.arange(slot_capacity, dtype=jnp.int32)[None, :]
        ).astype(jnp.float32)
        weighted = owner_match * slot_id.astype(jnp.float32)[:, None]
        requests_out = jnp.einsum(
            "io,is->os",
            weighted,
            slot_onehot,
            precision=lax.Precision.HIGHEST,
            preferred_element_type=jnp.float32,
        )
        outgoing.append(requests_out.astype(jnp.int32))
        layouts.append((item_row_codes, is_cold, flat_index, slot_capacity))
    wanted_all = jnp.concatenate(outgoing, axis=1)
    cold_rows = jnp.take(
        cold_item_table,
        lax.all_to_all(wanted_all, "table", split_axis=0, concat_axis=0, tiled=True),
        axis=0,
    ).astype(jnp.bfloat16)
    fetched = lax.all_to_all(cold_rows, "table", split_axis=0, concat_axis=0, tiled=True)
    results = []
    column_start = 0
    for item_row_codes, is_cold, flat_index, slot_capacity in layouts:
        flat_rows = fetched[:, column_start : column_start + slot_capacity].reshape(
            table_row_count * slot_capacity, fetched.shape[2]
        )
        picked = jnp.take(flat_rows, jnp.where(is_cold, flat_index, 0), axis=0)
        hot_rows = jnp.take(hot_item_table, jnp.where(is_cold, 0, item_row_codes), axis=0).astype(
            jnp.bfloat16
        )
        results.append(jnp.where(is_cold[:, None], picked, hot_rows))
        column_start = column_start + slot_capacity
    return results


def body(
    hot_item_table, cold_item_table, hist_rows, cand_rows, w_query, w_key, w_first, w_second, w_out
):
    table_row_count = lax.axis_size("table")
    requests, h_dev = hist_rows.shape
    c_dev = cand_rows.shape[1]
    width = hot_item_table.shape[1]
    cap_h = max(2, requests * h_dev // table_row_count)
    cap_c = max(2, requests * c_dev // table_row_count)
    history_emb, candidate_emb = gather_owner_rows(
        [hist_rows.reshape(-1), cand_rows.reshape(-1)],
        [cap_h, cap_c],
        hot_item_table,
        cold_item_table,
        table_row_count,
    )
    candidate_bf = candidate_emb.reshape(requests, c_dev, width)
    queries = jnp.einsum(
        "rce,ea->rca", candidate_bf, w_query, preferred_element_type=jnp.float32
    ).astype(jnp.bfloat16)
    score_scale = 1.0 / math.sqrt(w_query.shape[1])
    history_bf = history_emb.reshape(requests, h_dev, width)
    shard_rows = lax.all_gather(history_bf, "score", axis=1, tiled=True)
    key_rows = jnp.einsum(
        "rhe,ea->rha", shard_rows, w_key, preferred_element_type=jnp.float32
    ).astype(jnp.bfloat16)
    logits = (
        jnp.einsum("rca,rha->rch", queries, key_rows, preferred_element_type=jnp.float32)
        * score_scale
    )
    weights = jax.nn.sigmoid(logits).astype(jnp.bfloat16)
    pooled_sum = jnp.einsum("rch,rhe->rce", weights, shard_rows, preferred_element_type=jnp.float32)
    pooled = (pooled_sum * (1.0 / math.sqrt(H))).astype(jnp.bfloat16)
    joined = jnp.concatenate([candidate_bf, pooled], axis=2).reshape(requests * c_dev, 2 * width)
    hidden = jnp.maximum(jnp.dot(joined, w_first, preferred_element_type=jnp.float32), 0.0).astype(
        jnp.bfloat16
    )
    hidden = jnp.maximum(
        jnp.dot(hidden, w_second[0], preferred_element_type=jnp.float32), 0.0
    ).astype(jnp.bfloat16)
    ranked = jnp.dot(hidden, w_out, preferred_element_type=jnp.float32)
    return ranked.reshape(requests, c_dev)


def solution(mesh):
    return jax.shard_map(
        body,
        mesh=mesh,
        in_specs=(
            P(),
            P("table", None),
            P("table", "score"),
            P("table", "score"),
            P(),
            P(),
            P(),
            P(),
            P(),
        ),
        out_specs=P("table", "score"),
        check_vma=False,
    )
```

profile of v0, /device:TPU:0, one launch (start us, length us, event | category | flops | bytes accessed | tf_op | source)
XLA Modules:
  0.0 134.3 jit_solution(15087299233577586099)
XLA Ops:
  6.5 0.0 copy-start
  6.5 0.9 broadcast_compare_fusion.1
  7.4 0.7 broadcast_add_fusion.1
  8.1 0.7 broadcast_compare_fusion
  8.8 0.7 broadcast_add_fusion
  9.5 0.1 convert_reduce_fusion.1
  9.7 0.1 fusion.49
  9.8 0.2 fusion.7
  10.0 0.7 copy.13
  10.8 0.1 convert_reduce_fusion
  10.9 0.1 fusion.48
  11.0 0.2 fusion.6
  11.2 0.7 copy.12
  12.0 2.1 %convolution_convert_fusion.3 = s32[16,128]{1,0:T(8,128)S(1)} fusion(s32[2048]{0:T(1024)S(1)} %convert_bitcast_fusion.1, f32[2048]{0:T(1024)S(1)} %get-tuple-element.16, s32[2048]{0:T(1024)S(1)} %get-tuple-element.8, pred[2048]{0:T(1024)(128)(4,1)S(1)} %get-tuple-element.9), kind=kOutput, calls=%fused_computation.23 | convolution fusion | flops 50694144 | bytes 34816 | tf_op jit(solution)/shard_map/io,is->os/dot_general | solution.py:58
  14.1 2.1 %convolution_convert_fusion.2 = s32[16,128]{1,0:T(8,128)S(1)} fusion(s32[2048]{0:T(1024)S(1)} %convert_bitcast_fusion, f32[2048]{0:T(1024)S(1)} %get-tuple-element.17, s32[2048]{0:T(1024)S(1)} %get-tuple-element.11, pred[2048]{0:T(1024)(128)(4,1)S(1)} %get-tuple-element.12), kind=kOutput, calls=%fused_computation.22 | convolution fusion | flops 50694144 | bytes 34816 | tf_op jit(solution)/shard_map/io,is->os/dot_general | solution.py:58
  16.2 15.4 %all_to_all.20 = s32[16,1,256]{2,1,0:T(1,128)S(1)} all-to-all(s32[16,1,256]{2,1,0:T(1,128)S(1)} %copy.10), channel_id=1, replica_groups=mesh['table'=16,'score'=2] {'table'}, dimensions={0} | all-to-all | bytes 32768 | tf_op jit(solution)/shard_map/all_to_all | solution.py:70
  31.7 0.0 copy-done.1
  31.7 14.2 %gather_fusion = bf16[4096,128]{1,0:T(8,128)(2,1)} fusion(f32[1024,128]{1,0:T(8,128)S(1)} %copy-done.1, s32[4096]{0:T(1024)S(1)} %broadcast_clamp_fusion), kind=kCustom, calls=%fused_computation.4 | custom fusion | bytes 2113536 | tf_op jit(solution)/shard_map/jit(_take)/gather | solution.py:68
  46.0 2.6 %select_convert_fusion = bf16[16,256,128]{2,1,0:T(8,128)(2,1)} fusion(bf16[16,256,128]{2,1,0:T(8,128)(2,1)} %bitcast.70, pred[16,256]{1,0:T(8,128)(4,1)S(1)} %compare_and_fusion), kind=kLoop, calls=%fused_computation.9 | loop fusion | flops 524288 | bytes 2101248 | tf_op jit(solution)/shard_map/convert_element_type | solution.py:72
  48.6 4.3 %all-to-all-start.1 = ((bf16[16,256,128]{2,1,0:T(8,128)(2,1)}), bf16[16,256,128]{2,1,0:T(8,128)(2,1)}, u32[]{:S(2)}, u32[]{:S(2)}) async-start(bf16[16,256,128]{2,1,0:T(8,128)(2,1)} %select_convert_fusion), calls=%async_computation.1 | async-start | bytes 2097152 | tf_op jit(solution)/shard_map/all_to_all | solution.py:73
  53.0 0.2 all-gather.2.cloned.1.call-start
  53.2 0.0 copy-done.2
  53.2 7.6 %gather_fusion.4 = bf16[2048,128]{1,0:T(8,128)(2,1)} fusion(f32[2048,128]{1,0:T(8,128)S(1)} %copy-done.2, s32[2048]{0:T(1024)S(1)} %get-tuple-element.15), kind=kCustom, calls=%fused_computation.3.clone | custom fusion | bytes 1056768 | tf_op jit(solution)/shard_map/jit(_take)/gather | solution.py:81
  60.8 15.4 %all-to-all-done.1 = bf16[16,256,128]{2,1,0:T(8,128)(2,1)} async-done(((bf16[16,256,128]{2,1,0:T(8,128)(2,1)}), bf16[16,256,128]{2,1,0:T(8,128)(2,1)}, u32[]{:S(2)}, u32[]{:S(2)}) %all-to-all-start.1) | async-done | bytes 1048608 | tf_op jit(solution)/shard_map/all_to_all | solution.py:73
  76.3 2.3 %fusion.61 = (bf16[16,128,128]{2,1,0:T(8,128)(2,1)}, bf16[16,128,128]{2,1,0:T(8,128)(2,1)}) fusion(bf16[16,256,128]{2,1,0:T(8,128)(2,1)} %all-to-all-done.1), kind=kLoop, calls=%fused_computation.131 | loop fusion | bytes 2097152 | tf_op jit(solution)/shard_map/slice | solution.py:77
  78.6 8.8 %gather_fusion.3 = bf16[2048,128]{1,0:T(8,128)(2,1)} fusion(bf16[2048,128]{1,0:T(8,128)(2,1)} %bitcast.69, s32[2048]{0:T(1024)S(1)} %get-tuple-element.19), kind=kCustom, calls=%fused_computation.2.clone | custom fusion | bytes 1056768 | tf_op jit(solution)/shard_map/jit(_take)/gather | solution.py:80
  87.3 4.0 %fusion.21 = bf16[2048,128]{1,0:T(8,128)(2,1)} fusion(bf16[2048,128]{1,0:T(8,128)(2,1)} %gather_fusion.4, bf16[2048,128]{1,0:T(8,128)(2,1)} %gather_fusion.3, pred[2048]{0:T(1024)(128)(4,1)S(1)} %compare_and_fusion.1, pred[2048]{0:T(1024)(128)(4,1)S(1)} %get-tuple-element.6, pred[2048]{0:T(1024)(128)(4,1)S(1)} %get-tuple-element.9), kind=kLoop, calls=%fused_computation.38 | loop fusion | flops 786432 | bytes 1579008 | tf_op jit(solution)/shard_map/jit(_where)/select_n | solution.py:84
  91.4 0.0 all-gather.2.cloned.1.call-update
  91.4 7.6 %gather_fusion.2 = bf16[2048,128]{1,0:T(8,128)(2,1)} fusion(f32[2048,128]{1,0:T(8,128)S(1)} %copy-done.2, s32[2048]{0:T(1024)S(1)} %get-tuple-element.18), kind=kCustom, calls=%fused_computation.1.clone | custom fusion | bytes 1056768 | tf_op jit(solution)/shard_map/jit(_take)/gather | solution.py:81
  99.0 0.0 copy-done.7
  99.0 0.0 copy-start.8
  99.1 6.9 %gather_fusion.1 = bf16[2048,128]{1,0:T(8,128)(2,1)S(1)} fusion(bf16[2048,128]{1,0:T(8,128)(2,1)} %bitcast.68, s32[2048]{0:T(1024)S(1)} %get-tuple-element.20), kind=kCustom, calls=%fused_computation.clone | custom fusion | bytes 1056768 | tf_op jit(solution)/shard_map/jit(_take)/gather | solution.py:80
  106.0 0.0 copy-done.3
  106.0 1.6 %fusion.20 = bf16[2048,128]{1,0:T(8,128)(2,1)S(1)} fusion(bf16[2048,128]{1,0:T(8,128)(2,1)S(1)} %copy-done.3, bf16[2048,128]{1,0:T(8,128)(2,1)S(1)} %gather_fusion.1, pred[2048]{0:T(1024)(128)(4,1)S(1)} %compare_and_fusion.3, pred[2048]{0:T(1024)(128)(4,1)S(1)} %get-tuple-element.10, pred[2048]{0:T(1024)(128)(4,1)S(1)} %get-tuple-element.12), kind=kLoop, calls=%fused_computation.37 | loop fusion | flops 786432 | bytes 1579008 | tf_op jit(solution)/shard_map/jit(_where)/select_n | solution.py:84
  107.6 0.0 copy-start.4
  107.6 0.8 copy-done.4
  108.4 0.0 copy-done.6
  108.4 0.3 convolution_convert_fusion.1
  108.7 0.0 copy-start.5
  108.7 0.0 all-gather.2.cloned.1.call-done
  108.7 0.0 copy-done.8
  108.7 4.0 %divide_convert_fusion = bf16[8,256,512]{2,1,0:T(8,128)(2,1)} fusion(bf16[8,256,128]{2,1,0:T(8,128)(2,1)S(1)} %convolution_convert_fusion.1, bf16[8,512,128]{2,1,0:T(8,128)(2,1)} %all-gather.2.cloned.1.call-done, bf16[128,128]{1,0:T(8,128)(2,1)S(1)} %copy-done.8), kind=kOutput, calls=%fused_computation.7 | convolution fusion | flops 408420352 | bytes 3702784 | tf_op jit(solution)/shard_map/rca,rha->rch/dot_general | solution.py:116
  112.8 2.5 %fusion.1 = bf16[8,256,128]{2,1,0:T(8,128)(2,1)S(1)} fusion(bf16[8,256,512]{2,1,0:T(8,128)(2,1)} %divide_convert_fusion, bf16[8,512,128]{2,1,0:T(8,128)(2,1)} %all-gather.2.cloned.1.call-done), kind=kOutput, calls=%fused_computation.13 | convolution fusion | flops 268959744 | bytes 3670016 | tf_op jit(solution)/shard_map/rch,rhe->rce/dot_general | solution.py:120
  115.4 0.0 copy-done
  115.4 0.0 copy-done.5
  115.4 8.1 %maximum_convert_fusion = bf16[2048,1024]{1,0:T(8,128)(2,1)} fusion(bf16[1,1024,1024]{2,1,0:T(8,128)(2,1)S(1)} %copy-done, bf16[256,1024]{1,0:T(8,128)(2,1)} %param.19, bf16[2048,128]{1,0:T(8,128)(2,1)S(1)} %bitcast.83, bf16[2048,128]{1,0:T(8,128)(2,1)S(1)} %copy-done.5), kind=kOutput, calls=%fused_computation.5 | convolution fusion | flops 5379194880 | bytes 7864320 | tf_op jit(solution)/shard_map/dot_general | solution.py:127
  123.5 3.4 %fusion.62 = f32[1,2048]{1,0:T(1,128)S(1)} fusion(bf16[2048,1024]{1,0:T(8,128)(2,1)} %maximum_convert_fusion, bf16[1024,1]{0,1:T(2,128)(2,1)S(1)} %reshape.312), kind=kOutput, calls=%fused_computation.132 | convolution fusion | flops 4194304 | bytes 4204544 | tf_op jit(solution)/shard_map/dot_general | solution.py:129
  126.9 0.6 reshape.255
  (25 shorter events, 0.3 us)
Async XLA Ops:
  6.5 108.8 %copy-start = (bf16[1,1024,1024]{2,1,0:T(8,128)(2,1)S(1)}, bf16[1,1024,1024]{2,1,0:T(8,128)(2,1)}, u32[]{:S(2)}) copy-start(bf16[1,1024,1024]{2,1,0:T(8,128)(2,1)} %param.20) | copy-start | bytes 6291460
  6.5 25.2 %copy-start.1 = (f32[1024,128]{1,0:T(8,128)S(1)}, f32[1024,128]{1,0:T(8,128)}, u32[]{:S(2)}) copy-start(f32[1024,128]{1,0:T(8,128)} %param.14) | copy-start | bytes 1572868
  46.0 7.2 %copy-start.2 = (f32[2048,128]{1,0:T(8,128)S(1)}, f32[2048,128]{1,0:T(8,128)}, u32[]{:S(2)}) copy-start(f32[2048,128]{1,0:T(8,128)} %param.13) | copy-start | bytes 3145732
  48.6 27.6 %all-to-all-start.1 = ((bf16[16,256,128]{2,1,0:T(8,128)(2,1)}), bf16[16,256,128]{2,1,0:T(8,128)(2,1)}, u32[]{:S(2)}, u32[]{:S(2)}) async-start(bf16[16,256,128]{2,1,0:T(8,128)(2,1)} %select_convert_fusion), calls=%async_computation.1 | async-start | bytes 2097152 | tf_op jit(solution)/shard_map/all_to_all | solution.py:73
  53.0 55.8 %all-gather.2.cloned.1.call-start = ((), (), s32[]{:S(2)}) async-start(), calls=%async_computation.2 | async-start | bytes 1572864 | tf_op jit(solution)/shard_map/all_gather | solution.py:111
  87.3 11.7 %copy-start.7 = (bf16[1024]{0:T(1024)(128)(2,1)S(1)}, bf16[1024]{0:T(1024)(128)(2,1)}, u32[]{:S(2)}) copy-start(bf16[1024]{0:T(1024)(128)(2,1)} %param.21) | copy-start | bytes 6148
  99.0 6.9 %copy-start.3 = (bf16[2048,128]{1,0:T(8,128)(2,1)S(1)}, bf16[2048,128]{1,0:T(8,128)(2,1)}, u32[]{:S(2)}) copy-start(bf16[2048,128]{1,0:T(8,128)(2,1)} %gather_fusion.2) | copy-start | bytes 1572868
  99.0 9.4 %copy-start.6 = (bf16[128,128]{1,0:T(8,128)(2,1)S(1)}, bf16[128,128]{1,0:T(8,128)(2,1)}, u32[]{:S(2)}) copy-start(bf16[128,128]{1,0:T(8,128)(2,1)} %param.17) | copy-start | bytes 98308
  99.0 9.7 %copy-start.8 = (bf16[128,128]{1,0:T(8,128)(2,1)S(1)}, bf16[128,128]{1,0:T(8,128)(2,1)}, u32[]{:S(2)}) copy-start(bf16[128,128]{1,0:T(8,128)(2,1)} %param.18) | copy-start | bytes 98308
  107.6 0.8 copy-start.4
  108.7 6.7 %copy-start.5 = (bf16[2048,128]{1,0:T(8,128)(2,1)S(1)}, bf16[2048,128]{1,0:T(8,128)(2,1)}, u32[]{:S(2)}) copy-start(bf16[2048,128]{1,0:T(8,128)(2,1)} %copy-done.4) | copy-start | bytes 1572868
Sparse Core Ops, SparseCore 0:
  91.5 9.2 all-gather.1
where the time goes:
time: 135 us; the launch traced here: 134 us
  local copies, waits for them, and re-layouts  50.4 us (37%)
  matrix products  23.2 us (17%)
  waiting for transfers between devices  15.5 us (11%)
  blocking collectives  15.4 us (11%)
  between operations  13.7 us (10%)
  other arithmetic  11.7 us (9%)
  starting transfers between devices  4.56 us (3%)
    gather x2, local copies, waits for them, and re-layouts, gather_owner_rows(): picked = jnp.take(flat_rows, jnp.where(is_cold, flat_index, 0), axis=0)  15.6 us
    all_to_all x1, blocking collectives, gather_owner_rows(): lax.all_to_all(wanted_all, 'table', split_axis=0, concat_axis=0, tiled=True)  15.4 us
    all_to_all x1, waiting for transfers between devices, gather_owner_rows(): lax.all_to_all(cold_rows, 'table', split_axis=0, concat_axis=0, tiled=True)  15.4 us
    gather x2, local copies, waits for them, and re-layouts, gather_owner_rows(): jnp.take(hot_item_table, jnp.where(is_cold, 0, item_row_codes), axis=0)  15.2 us
    gather x1, local copies, waits for them, and re-layouts, gather_owner_rows(): jnp.take(cold_item_table, lax.all_to_all(wanted_all, 'table', split_axis=...  14.2 us
    dot_general x1, matrix products, body(): jnp.dot(hidden, w_second[0], preferred_element_type=jnp.float32)  8.14 us
    select_n x2, other arithmetic, gather_owner_rows(): results.append(jnp.where(is_cold[:, None], picked, hot_rows))  5.69 us
    all_to_all x1, starting transfers between devices, gather_owner_rows(): lax.all_to_all(cold_rows, 'table', split_axis=0, concat_axis=0, tiled=True)  4.34 us
  transfers between devices with their start and end apart: 2, of which 1 were waited for; matrix products, arithmetic and copies ran while one was open for 18% of the time, Pallas kernels for 0%

commit v1 on v0

--- a/solution.py
+++ b/solution.py
@@ -7,6 +7,29 @@
 H = 512
 HOT = 2048
 COLD_DEV = 1024
+
+
+def split_up(value, dim, count):
+    shape = value.shape
+    parts = value.reshape(*shape[:dim], count, shape[dim] // count, *shape[dim + 1 :])
+    return jnp.moveaxis(parts, dim, 0)
+
+
+def joined_along(blocks, dim):
+    shape = list(blocks.shape[1:])
+    shape[dim] *= blocks.shape[0]
+    return jnp.moveaxis(blocks, 0, dim).reshape(shape)
+
+
+def exchange_directly(x, axis, split_dim, concat_dim):
+    size, mine = (lax.axis_size(axis), lax.axis_index(axis))
+    blocks = split_up(x, split_dim, size)
+    gathered = [blocks[mine]]
+    for step in range(1, size):
+        sent = blocks[(mine + step) % size]
+        gathered.append(lax.ppermute(sent, axis, [(i, (i + step) % size) for i in range(size)]))
+    blocks = jnp.stack(gathered)[(mine - jnp.arange(size)) % size]
+    return joined_along(blocks, concat_dim)
 
 
 def owner_positions(owner_match):
@@ -66,9 +89,7 @@
         layouts.append((item_row_codes, is_cold, flat_index, slot_capacity))
     wanted_all = jnp.concatenate(outgoing, axis=1)
     cold_rows = jnp.take(
-        cold_item_table,
-        lax.all_to_all(wanted_all, "table", split_axis=0, concat_axis=0, tiled=True),
-        axis=0,
+        cold_item_table, exchange_directly(wanted_all, "table", 0, 0), axis=0
     ).astype(jnp.bfloat16)
     fetched = lax.all_to_all(cold_rows, "table", split_axis=0, concat_axis=0, tiled=True)
     results = []

time: 135 us -> 151 us (1.12)
  starting transfers between devices: 4.56 us -> 32.8 us
  blocking collectives: 15.4 us -> 0 us
  waiting for transfers between devices: 15.5 us -> 17.7 us
    ppermute x0 -> x15, starting transfers between devices: none -> 28 us  [exchange_directly(): lax.ppermute(sent, axis, [(i, (i + step) % size) for i in range(size)])]
    all_to_all x1 -> x0, blocking collectives: 15.4 us -> none  [gather_owner_rows(): lax.all_to_all(wanted_all, 'table', split_axis=0, concat_axis=0, tiled=True)]
    ppermute x0 -> x15, waiting for transfers between devices: none -> 4.86 us  [exchange_directly(): lax.ppermute(sent, axis, [(i, (i + step) % size) for i in range(size)])]
    all_to_all x1, waiting for transfers between devices: 15.4 us -> 12.8 us  [gather_owner_rows(): lax.all_to_all(cold_rows, 'table', split_axis=0, concat_axis=0, tiled=True)]
    gather x1 -> x2, local copies, waits for them, and re-layouts: 14.2 us -> 14.9 us  [the longest x1 14.3 us: gather_owner_rows(): jnp.take(cold_item_table, exchange_directly(wanted_all, 'table', 0, 0), a...]
  transfers between devices with their start and end apart: 2 -> 17, of which waited for: 1 -> 5; matrix products, arithmetic and copies ran while one was open for 18% -> 16% of each run, Pallas kernels for 0% -> 0%
where the time goes in v1:
time: 151 us; the launch traced here: 150 us
  local copies, waits for them, and re-layouts  51.1 us (34%)
  starting transfers between devices  32.8 us (22%)
  matrix products  23.2 us (15%)
  waiting for transfers between devices  17.7 us (12%)
  between operations  13.7 us (9%)
  other arithmetic  11.7 us (8%)
    ppermute x15, starting transfers between devices, exchange_directly(): lax.ppermute(sent, axis, [(i, (i + step) % size) for i in range(size)])  28 us
    gather x2, local copies, waits for them, and re-layouts, gather_owner_rows(): picked = jnp.take(flat_rows, jnp.where(is_cold, flat_index, 0), axis=0)  15.6 us
    gather x2, local copies, waits for them, and re-layouts, gather_owner_rows(): jnp.take(hot_item_table, jnp.where(is_cold, 0, item_row_codes), axis=0)  15.4 us
    gather x1, local copies, waits for them, and re-layouts, gather_owner_rows(): jnp.take(cold_item_table, exchange_directly(wanted_all, 'table', 0, 0), a...  14.3 us
    all_to_all x1, waiting for transfers between devices, gather_owner_rows(): lax.all_to_all(cold_rows, 'table', split_axis=0, concat_axis=0, tiled=True)  12.8 us
    dot_general x1, matrix products, body(): jnp.dot(hidden, w_second[0], preferred_element_type=jnp.float32)  8.13 us
    select_n x2, other arithmetic, gather_owner_rows(): results.append(jnp.where(is_cold[:, None], picked, hot_rows))  5.72 us
    ppermute x15, waiting for transfers between devices, exchange_directly(): lax.ppermute(sent, axis, [(i, (i + step) % size) for i in range(size)])  4.86 us
  transfers between devices with their start and end apart: 17, of which 5 were waited for; matrix products, arithmetic and copies ran while one was open for 16% of the time, Pallas kernels for 0%

profile of v1, /device:TPU:0, one launch (start us, length us, event | category | flops | bytes accessed | tf_op | source)
XLA Modules:
  0.0 150.2 jit_solution(11914817156686161932)
XLA Ops:
  6.5 0.9 broadcast_compare_fusion.1
  7.4 0.7 broadcast_add_fusion.1
  8.1 0.7 broadcast_compare_fusion
  8.8 0.7 broadcast_add_fusion
  9.8 0.2 fusion.7
  10.0 0.7 copy.11
  10.9 0.1 fusion.49
  11.0 0.2 fusion.6
  11.2 0.7 copy.10
  12.0 2.1 %convolution_convert_fusion.3 = s32[16,128]{1,0:T(8,128)S(1)} fusion(s32[2048]{0:T(1024)S(1)} %convert_bitcast_fusion.1, f32[2048]{0:T(1024)S(1)} %get-tuple-element.32, s32[2048]{0:T(1024)S(1)} %get-tuple-element.8, pred[2048]{0:T(1024)(128)(4,1)S(1)} %get-tuple-element.9), kind=kOutput, calls=%fused_computation.24 | convolution fusion | flops 50694144 | bytes 34816 | tf_op jit(solution)/shard_map/io,is->os/dot_general | solution.py:81
  14.1 2.1 %convolution_convert_fusion.2 = s32[16,128]{1,0:T(8,128)S(1)} fusion(s32[2048]{0:T(1024)S(1)} %convert_bitcast_fusion, f32[2048]{0:T(1024)S(1)} %get-tuple-element.33, s32[2048]{0:T(1024)S(1)} %get-tuple-element.11, pred[2048]{0:T(1024)(128)(4,1)S(1)} %get-tuple-element.12), kind=kOutput, calls=%fused_computation.23 | convolution fusion | flops 50694144 | bytes 34816 | tf_op jit(solution)/shard_map/io,is->os/dot_general | solution.py:81
  16.2 5.0 %collective-permute-start.9 = (s32[1,256]{1,0:T(1,128)S(1)}, s32[1,256]{1,0:T(1,128)S(1)}, u32[]{:S(2)}, u32[]{:S(2)}) collective-permute-start(s32[1,256]{1,0:T(1,128)S(1)} %get-tuple-element.28), channel_id=1, source_target_pairs={{0,20},{2,22},{4,24},{6,26},{8,28},{10,30},{12,0},{14,2},{16,4},{1... | collective-permute-start | bytes 3080 | tf_op jit(solution)/shard_map/ppermute | solution.py:30
  21.3 1.3 collective-permute-start.10
  22.6 1.4 collective-permute-start.11
  24.0 2.7 %collective-permute-start.12 = (s32[1,256]{1,0:T(1,128)S(1)}, s32[1,256]{1,0:T(1,128)S(1)}, u32[]{:S(2)}, u32[]{:S(2)}) collective-permute-start(s32[1,256]{1,0:T(1,128)S(1)} %get-tuple-element.27), channel_id=1, source_target_pairs={{0,26},{2,28},{4,30},{6,0},{8,2},{10,4},{12,6},{14,8},{16,10},{18,... | collective-permute-start | bytes 3080 | tf_op jit(solution)/shard_map/ppermute | solution.py:30
  26.7 1.2 collective-permute-start.4
  27.9 1.2 collective-permute-start.5
  29.2 2.1 %collective-permute-start.6 = (s32[1,256]{1,0:T(1,128)S(1)}, s32[1,256]{1,0:T(1,128)S(1)}, u32[]{:S(2)}, u32[]{:S(2)}) collective-permute-start(s32[1,256]{1,0:T(1,128)S(1)} %get-tuple-element.24), channel_id=1, source_target_pairs={{0,14},{2,16},{4,18},{6,20},{8,22},{10,24},{12,26},{14,28},{16,30}... | collective-permute-start | bytes 3080 | tf_op jit(solution)/shard_map/ppermute | solution.py:30
  31.3 1.3 collective-permute-start.7
  32.5 2.2 %collective-permute-start.8 = (s32[1,256]{1,0:T(1,128)S(1)}, s32[1,256]{1,0:T(1,128)S(1)}, u32[]{:S(2)}, u32[]{:S(2)}) collective-permute-start(s32[1,256]{1,0:T(1,128)S(1)} %get-tuple-element.26), channel_id=1, source_target_pairs={{0,18},{2,20},{4,22},{6,24},{8,26},{10,28},{12,30},{14,0},{16,2},{... | collective-permute-start | bytes 3080 | tf_op jit(solution)/shard_map/ppermute | solution.py:30
  34.7 5.5 %collective-permute-start.13 = (s32[1,256]{1,0:T(1,128)S(1)}, s32[1,256]{1,0:T(1,128)S(1)}, u32[]{:S(2)}, u32[]{:S(2)}) collective-permute-start(s32[1,256]{1,0:T(1,128)S(1)} %get-tuple-element.21), channel_id=1, source_target_pairs={{0,28},{2,30},{4,0},{6,2},{8,4},{10,6},{12,8},{14,10},{16,12},{18,... | collective-permute-start | bytes 3080 | tf_op jit(solution)/shard_map/ppermute | solution.py:30
  40.2 0.6 collective-permute-start.14
  40.8 1.5 collective-permute-start
  42.3 1.6 %collective-permute-start.2 = (s32[1,256]{1,0:T(1,128)S(1)}, s32[1,256]{1,0:T(1,128)S(1)}, u32[]{:S(2)}, u32[]{:S(2)}) collective-permute-start(s32[1,256]{1,0:T(1,128)S(1)} %get-tuple-element.19), channel_id=1, source_target_pairs={{0,6},{2,8},{4,10},{6,12},{8,14},{10,16},{12,18},{14,20},{16,22},{... | collective-permute-start | bytes 3080 | tf_op jit(solution)/shard_map/ppermute | solution.py:30
  43.8 0.5 collective-permute-start.3
  44.4 3.6 %collective-permute-done = s32[1,256]{1,0:T(1,128)S(1)} collective-permute-done((s32[1,256]{1,0:T(1,128)S(1)}, s32[1,256]{1,0:T(1,128)S(1)}, u32[]{:S(2)}, u32[]{:S(2)}) %collective-permute-start) | collective-permute-done | bytes 1056 | tf_op jit(solution)/shard_map/ppermute | solution.py:30
  47.9 0.6 collective-permute-done.1
  48.6 0.6 collective-permute-done.3
  49.3 0.6 gather_fusion
  49.9 14.3 %gather_fusion.1 = bf16[4096,128]{1,0:T(8,128)(2,1)} fusion(f32[1024,128]{1,0:T(8,128)S(1)} %copy-done.1, s32[4096]{0:T(1024)S(1)} %broadcast_clamp_fusion), kind=kCustom, calls=%fused_computation.5 | custom fusion | bytes 2113536 | tf_op jit(solution)/shard_map/jit(_take)/gather | solution.py:91
  64.3 2.6 %select_convert_fusion = bf16[16,256,128]{2,1,0:T(8,128)(2,1)} fusion(bf16[16,256,128]{2,1,0:T(8,128)(2,1)} %bitcast.87, pred[16,256]{1,0:T(8,128)(4,1)S(1)} %compare_and_fusion), kind=kLoop, calls=%fused_computation.10 | loop fusion | flops 524288 | bytes 2101248 | tf_op jit(solution)/shard_map/convert_element_type | solution.py:93
  66.9 4.6 %all-to-all-start = ((bf16[16,256,128]{2,1,0:T(8,128)(2,1)}), bf16[16,256,128]{2,1,0:T(8,128)(2,1)}, u32[]{:S(2)}, u32[]{:S(2)}) async-start(bf16[16,256,128]{2,1,0:T(8,128)(2,1)} %select_convert_fusion), calls=%async_computation | async-start | bytes 2097152 | tf_op jit(solution)/shard_map/all_to_all | solution.py:94
  71.4 0.2 all-gather.2.cloned.1.call-start
  71.7 7.7 %gather_fusion.5 = bf16[2048,128]{1,0:T(8,128)(2,1)} fusion(f32[2048,128]{1,0:T(8,128)S(1)} %copy-done.2, s32[2048]{0:T(1024)S(1)} %get-tuple-element.31), kind=kCustom, calls=%fused_computation.3.clone | custom fusion | bytes 1056768 | tf_op jit(solution)/shard_map/jit(_take)/gather | solution.py:102
  79.4 12.8 %all-to-all-done = bf16[16,256,128]{2,1,0:T(8,128)(2,1)} async-done(((bf16[16,256,128]{2,1,0:T(8,128)(2,1)}), bf16[16,256,128]{2,1,0:T(8,128)(2,1)}, u32[]{:S(2)}, u32[]{:S(2)}) %all-to-all-start) | async-done | bytes 1048608 | tf_op jit(solution)/shard_map/all_to_all | solution.py:94
  92.2 2.3 %fusion.81 = (bf16[16,128,128]{2,1,0:T(8,128)(2,1)}, bf16[16,128,128]{2,1,0:T(8,128)(2,1)}) fusion(bf16[16,256,128]{2,1,0:T(8,128)(2,1)} %all-to-all-done), kind=kLoop, calls=%fused_computation.188 | loop fusion | bytes 2097152 | tf_op jit(solution)/shard_map/slice | solution.py:98
  94.5 8.8 %gather_fusion.4 = bf16[2048,128]{1,0:T(8,128)(2,1)} fusion(bf16[2048,128]{1,0:T(8,128)(2,1)} %bitcast.86, s32[2048]{0:T(1024)S(1)} %get-tuple-element.35), kind=kCustom, calls=%fused_computation.2.clone | custom fusion | bytes 1056768 | tf_op jit(solution)/shard_map/jit(_take)/gather | solution.py:101
  103.3 4.1 %fusion.21 = bf16[2048,128]{1,0:T(8,128)(2,1)} fusion(bf16[2048,128]{1,0:T(8,128)(2,1)} %gather_fusion.5, bf16[2048,128]{1,0:T(8,128)(2,1)} %gather_fusion.4, pred[2048]{0:T(1024)(128)(4,1)S(1)} %compare_and_fusion.1, pred[2048]{0:T(1024)(128)(4,1)S(1)} %get-tuple-element.6, pred[2048]{0:T(1024)(128)(4,1)S(1)} %get-tuple-element.9), kind=kLoop, calls=%fused_computation.39 | loop fusion | flops 786432 | bytes 1579008 | tf_op jit(solution)/shard_map/jit(_where)/select_n | solution.py:105
  107.4 7.7 %gather_fusion.3 = bf16[2048,128]{1,0:T(8,128)(2,1)} fusion(f32[2048,128]{1,0:T(8,128)S(1)} %copy-done.2, s32[2048]{0:T(1024)S(1)} %get-tuple-element.34), kind=kCustom, calls=%fused_computation.1.clone | custom fusion | bytes 1056768 | tf_op jit(solution)/shard_map/jit(_take)/gather | solution.py:102
  115.1 6.7 %gather_fusion.2 = bf16[2048,128]{1,0:T(8,128)(2,1)S(1)} fusion(bf16[2048,128]{1,0:T(8,128)(2,1)} %bitcast.85, s32[2048]{0:T(1024)S(1)} %get-tuple-element.36), kind=kCustom, calls=%fused_computation.clone | custom fusion | bytes 1056768 | tf_op jit(solution)/shard_map/jit(_take)/gather | solution.py:101
  121.9 1.6 %fusion.20 = bf16[2048,128]{1,0:T(8,128)(2,1)S(1)} fusion(bf16[2048,128]{1,0:T(8,128)(2,1)S(1)} %copy-done.3, bf16[2048,128]{1,0:T(8,128)(2,1)S(1)} %gather_fusion.2, pred[2048]{0:T(1024)(128)(4,1)S(1)} %compare_and_fusion.3, pred[2048]{0:T(1024)(128)(4,1)S(1)} %get-tuple-element.10, pred[2048]{0:T(1024)(128)(4,1)S(1)} %get-tuple-element.12), kind=kLoop, calls=%fused_computation.38 | loop fusion | flops 786432 | bytes 1579008 | tf_op jit(solution)/shard_map/jit(_where)/select_n | solution.py:105
  123.6 0.8 copy-done.4
  124.3 0.3 convolution_convert_fusion.1
  124.7 4.0 %divide_convert_fusion = bf16[8,256,512]{2,1,0:T(8,128)(2,1)} fusion(bf16[8,256,128]{2,1,0:T(8,128)(2,1)S(1)} %convolution_convert_fusion.1, bf16[8,512,128]{2,1,0:T(8,128)(2,1)} %all-gather.2.cloned.1.call-done, bf16[128,128]{1,0:T(8,128)(2,1)S(1)} %copy-done.8), kind=kOutput, calls=%fused_computation.8 | convolution fusion | flops 408420352 | bytes 3702784 | tf_op jit(solution)/shard_map/rca,rha->rch/dot_general | solution.py:137
  128.7 2.5 %fusion.1 = bf16[8,256,128]{2,1,0:T(8,128)(2,1)S(1)} fusion(bf16[8,256,512]{2,1,0:T(8,128)(2,1)} %divide_convert_fusion, bf16[8,512,128]{2,1,0:T(8,128)(2,1)} %all-gather.2.cloned.1.call-done), kind=kOutput, calls=%fused_computation.14 | convolution fusion | flops 268959744 | bytes 3670016 | tf_op jit(solution)/shard_map/rch,rhe->rce/dot_general | solution.py:141
  131.3 8.1 %maximum_convert_fusion = bf16[2048,1024]{1,0:T(8,128)(2,1)} fusion(bf16[1,1024,1024]{2,1,0:T(8,128)(2,1)S(1)} %copy-done, bf16[256,1024]{1,0:T(8,128)(2,1)} %param.19, bf16[2048,128]{1,0:T(8,128)(2,1)S(1)} %bitcast.116, bf16[2048,128]{1,0:T(8,128)(2,1)S(1)} %copy-done.5), kind=kOutput, calls=%fused_computation.6 | convolution fusion | flops 5379194880 | bytes 7864320 | tf_op jit(solution)/shard_map/dot_general | solution.py:148
  139.4 3.4 %fusion.82 = f32[1,2048]{1,0:T(1,128)S(1)} fusion(bf16[2048,1024]{1,0:T(8,128)(2,1)} %maximum_convert_fusion, bf16[1024,1]{0,1:T(2,128)(2,1)S(1)} %reshape.410), kind=kOutput, calls=%fused_computation.189 | convolution fusion | flops 4194304 | bytes 4204544 | tf_op jit(solution)/shard_map/dot_general | solution.py:150
  142.8 0.6 reshape.341
  (59 shorter events, 0.8 us)
Async XLA Ops:
  6.5 124.7 %copy-start = (bf16[1,1024,1024]{2,1,0:T(8,128)(2,1)S(1)}, bf16[1,1024,1024]{2,1,0:T(8,128)(2,1)}, u32[]{:S(2)}) copy-start(bf16[1,1024,1024]{2,1,0:T(8,128)(2,1)} %param.20) | copy-start | bytes 6291460
  6.5 43.4 %copy-start.1 = (f32[1024,128]{1,0:T(8,128)S(1)}, f32[1024,128]{1,0:T(8,128)}, u32[]{:S(2)}) copy-start(f32[1024,128]{1,0:T(8,128)} %param.14) | copy-start | bytes 1572868
  16.2 11.7 %collective-permute-start.9 = (s32[1,256]{1,0:T(1,128)S(1)}, s32[1,256]{1,0:T(1,128)S(1)}, u32[]{:S(2)}, u32[]{:S(2)}) collective-permute-start(s32[1,256]{1,0:T(1,128)S(1)} %get-tuple-element.28), channel_id=1, source_target_pairs={{0,20},{2,22},{4,24},{6,26},{8,28},{10,30},{12,0},{14,2},{16,4},{1... | collective-permute-start | bytes 3080 | tf_op jit(solution)/shard_map/ppermute | solution.py:30
  21.3 7.9 %collective-permute-start.10 = (s32[1,256]{1,0:T(1,128)S(1)}, s32[1,256]{1,0:T(1,128)S(1)}, u32[]{:S(2)}, u32[]{:S(2)}) collective-permute-start(s32[1,256]{1,0:T(1,128)S(1)} %get-tuple-element.29), channel_id=1, source_target_pairs={{0,22},{2,24},{4,26},{6,28},{8,30},{10,0},{12,2},{14,4},{16,6},{18... | collective-permute-start | bytes 3080 | tf_op jit(solution)/shard_map/ppermute | solution.py:30
  22.6 8.7 %collective-permute-start.11 = (s32[1,256]{1,0:T(1,128)S(1)}, s32[1,256]{1,0:T(1,128)S(1)}, u32[]{:S(2)}, u32[]{:S(2)}) collective-permute-start(s32[1,256]{1,0:T(1,128)S(1)} %get-tuple-element.30), channel_id=1, source_target_pairs={{0,24},{2,26},{4,28},{6,30},{8,0},{10,2},{12,4},{14,6},{16,8},{18,... | collective-permute-start | bytes 3080 | tf_op jit(solution)/shard_map/ppermute | solution.py:30
  24.0 8.6 %collective-permute-start.12 = (s32[1,256]{1,0:T(1,128)S(1)}, s32[1,256]{1,0:T(1,128)S(1)}, u32[]{:S(2)}, u32[]{:S(2)}) collective-permute-start(s32[1,256]{1,0:T(1,128)S(1)} %get-tuple-element.27), channel_id=1, source_target_pairs={{0,26},{2,28},{4,30},{6,0},{8,2},{10,4},{12,6},{14,8},{16,10},{18,... | collective-permute-start | bytes 3080 | tf_op jit(solution)/shard_map/ppermute | solution.py:30
  26.7 8.0 %collective-permute-start.4 = (s32[1,256]{1,0:T(1,128)S(1)}, s32[1,256]{1,0:T(1,128)S(1)}, u32[]{:S(2)}, u32[]{:S(2)}) collective-permute-start(s32[1,256]{1,0:T(1,128)S(1)} %get-tuple-element.22), channel_id=1, source_target_pairs={{0,10},{2,12},{4,14},{6,16},{8,18},{10,20},{12,22},{14,24},{16,26}... | collective-permute-start | bytes 3080 | tf_op jit(solution)/shard_map/ppermute | solution.py:30
  27.9 12.2 %collective-permute-start.5 = (s32[1,256]{1,0:T(1,128)S(1)}, s32[1,256]{1,0:T(1,128)S(1)}, u32[]{:S(2)}, u32[]{:S(2)}) collective-permute-start(s32[1,256]{1,0:T(1,128)S(1)} %get-tuple-element.23), channel_id=1, source_target_pairs={{0,12},{2,14},{4,16},{6,18},{8,20},{10,22},{12,24},{14,26},{16,28}... | collective-permute-start | bytes 3080 | tf_op jit(solution)/shard_map/ppermute | solution.py:30
  29.2 11.6 %collective-permute-start.6 = (s32[1,256]{1,0:T(1,128)S(1)}, s32[1,256]{1,0:T(1,128)S(1)}, u32[]{:S(2)}, u32[]{:S(2)}) collective-permute-start(s32[1,256]{1,0:T(1,128)S(1)} %get-tuple-element.24), channel_id=1, source_target_pairs={{0,14},{2,16},{4,18},{6,20},{8,22},{10,24},{12,26},{14,28},{16,30}... | collective-permute-start | bytes 3080 | tf_op jit(solution)/shard_map/ppermute | solution.py:30
  31.3 11.0 %collective-permute-start.7 = (s32[1,256]{1,0:T(1,128)S(1)}, s32[1,256]{1,0:T(1,128)S(1)}, u32[]{:S(2)}, u32[]{:S(2)}) collective-permute-start(s32[1,256]{1,0:T(1,128)S(1)} %get-tuple-element.25), channel_id=1, source_target_pairs={{0,16},{2,18},{4,20},{6,22},{8,24},{10,26},{12,28},{14,30},{16,0},... | collective-permute-start | bytes 3080 | tf_op jit(solution)/shard_map/ppermute | solution.py:30
  32.5 9.7 %collective-permute-start.8 = (s32[1,256]{1,0:T(1,128)S(1)}, s32[1,256]{1,0:T(1,128)S(1)}, u32[]{:S(2)}, u32[]{:S(2)}) collective-permute-start(s32[1,256]{1,0:T(1,128)S(1)} %get-tuple-element.26), channel_id=1, source_target_pairs={{0,18},{2,20},{4,22},{6,24},{8,26},{10,28},{12,30},{14,0},{16,2},{... | collective-permute-start | bytes 3080 | tf_op jit(solution)/shard_map/ppermute | solution.py:30
  34.7 9.1 %collective-permute-start.13 = (s32[1,256]{1,0:T(1,128)S(1)}, s32[1,256]{1,0:T(1,128)S(1)}, u32[]{:S(2)}, u32[]{:S(2)}) collective-permute-start(s32[1,256]{1,0:T(1,128)S(1)} %get-tuple-element.21), channel_id=1, source_target_pairs={{0,28},{2,30},{4,0},{6,2},{8,4},{10,6},{12,8},{14,10},{16,12},{18,... | collective-permute-start | bytes 3080 | tf_op jit(solution)/shard_map/ppermute | solution.py:30
  40.2 4.2 %collective-permute-start.14 = (s32[1,256]{1,0:T(1,128)S(1)}, s32[1,256]{1,0:T(1,128)S(1)}, u32[]{:S(2)}, u32[]{:S(2)}) collective-permute-start(s32[1,256]{1,0:T(1,128)S(1)} %get-tuple-element.15), channel_id=1, source_target_pairs={{0,30},{2,0},{4,2},{6,4},{8,6},{10,8},{12,10},{14,12},{16,14},{18,... | collective-permute-start | bytes 3080 | tf_op jit(solution)/shard_map/ppermute | solution.py:30
  40.8 7.2 %collective-permute-start = (s32[1,256]{1,0:T(1,128)S(1)}, s32[1,256]{1,0:T(1,128)S(1)}, u32[]{:S(2)}, u32[]{:S(2)}) collective-permute-start(s32[1,256]{1,0:T(1,128)S(1)} %get-tuple-element.17), channel_id=1, source_target_pairs={{0,2},{2,4},{4,6},{6,8},{8,10},{10,12},{12,14},{14,16},{16,18},{18... | collective-permute-start | bytes 3080 | tf_op jit(solution)/shard_map/ppermute | solution.py:30
  42.3 6.3 %collective-permute-start.1 = (s32[1,256]{1,0:T(1,128)S(1)}, s32[1,256]{1,0:T(1,128)S(1)}, u32[]{:S(2)}, u32[]{:S(2)}) collective-permute-start(s32[1,256]{1,0:T(1,128)S(1)} %get-tuple-element.18), channel_id=1, source_target_pairs={{0,4},{2,6},{4,8},{6,10},{8,12},{10,14},{12,16},{14,18},{16,20},{1... | collective-permute-start | bytes 3080 | tf_op jit(solution)/shard_map/ppermute | solution.py:30
  42.3 6.3 %collective-permute-start.2 = (s32[1,256]{1,0:T(1,128)S(1)}, s32[1,256]{1,0:T(1,128)S(1)}, u32[]{:S(2)}, u32[]{:S(2)}) collective-permute-start(s32[1,256]{1,0:T(1,128)S(1)} %get-tuple-element.19), channel_id=1, source_target_pairs={{0,6},{2,8},{4,10},{6,12},{8,14},{10,16},{12,18},{14,20},{16,22},{... | collective-permute-start | bytes 3080 | tf_op jit(solution)/shard_map/ppermute | solution.py:30
  43.8 5.4 %collective-permute-start.3 = (s32[1,256]{1,0:T(1,128)S(1)}, s32[1,256]{1,0:T(1,128)S(1)}, u32[]{:S(2)}, u32[]{:S(2)}) collective-permute-start(s32[1,256]{1,0:T(1,128)S(1)} %get-tuple-element.20), channel_id=1, source_target_pairs={{0,8},{2,10},{4,12},{6,14},{8,16},{10,18},{12,20},{14,22},{16,24},... | collective-permute-start | bytes 3080 | tf_op jit(solution)/shard_map/ppermute | solution.py:30
  64.3 7.4 %copy-start.2 = (f32[2048,128]{1,0:T(8,128)S(1)}, f32[2048,128]{1,0:T(8,128)}, u32[]{:S(2)}) copy-start(f32[2048,128]{1,0:T(8,128)} %param.13) | copy-start | bytes 3145732
  66.9 25.3 %all-to-all-start = ((bf16[16,256,128]{2,1,0:T(8,128)(2,1)}), bf16[16,256,128]{2,1,0:T(8,128)(2,1)}, u32[]{:S(2)}, u32[]{:S(2)}) async-start(bf16[16,256,128]{2,1,0:T(8,128)(2,1)} %select_convert_fusion), calls=%async_computation | async-start | bytes 2097152 | tf_op jit(solution)/shard_map/all_to_all | solution.py:94
  71.4 53.2 %all-gather.2.cloned.1.call-start = ((), (), s32[]{:S(2)}) async-start(), calls=%async_computation.1 | async-start | bytes 1572864 | tf_op jit(solution)/shard_map/all_gather | solution.py:132
  103.3 11.8 %copy-start.7 = (bf16[1024]{0:T(1024)(128)(2,1)S(1)}, bf16[1024]{0:T(1024)(128)(2,1)}, u32[]{:S(2)}) copy-start(bf16[1024]{0:T(1024)(128)(2,1)} %param.21) | copy-start | bytes 6148
  115.1 6.8 %copy-start.3 = (bf16[2048,128]{1,0:T(8,128)(2,1)S(1)}, bf16[2048,128]{1,0:T(8,128)(2,1)}, u32[]{:S(2)}) copy-start(bf16[2048,128]{1,0:T(8,128)(2,1)} %gather_fusion.3) | copy-start | bytes 1572868
  115.1 9.2 %copy-start.6 = (bf16[128,128]{1,0:T(8,128)(2,1)S(1)}, bf16[128,128]{1,0:T(8,128)(2,1)}, u32[]{:S(2)}) copy-start(bf16[128,128]{1,0:T(8,128)(2,1)} %param.17) | copy-start | bytes 98308
  115.1 9.6 %copy-start.8 = (bf16[128,128]{1,0:T(8,128)(2,1)S(1)}, bf16[128,128]{1,0:T(8,128)(2,1)}, u32[]{:S(2)}) copy-start(bf16[128,128]{1,0:T(8,128)(2,1)} %param.18) | copy-start | bytes 98308
  123.6 0.8 copy-start.4
  124.6 6.6 %copy-start.5 = (bf16[2048,128]{1,0:T(8,128)(2,1)S(1)}, bf16[2048,128]{1,0:T(8,128)(2,1)}, u32[]{:S(2)}) copy-start(bf16[2048,128]{1,0:T(8,128)(2,1)} %copy-done.4) | copy-start | bytes 1572868
Sparse Core Ops, SparseCore 0:
  107.5 8.2 all-gather.1
